TPU v7x, 32 devices: a whole 2x2x4 slice. The times are simulated.
32 devices in a mesh: groups: 2 (over y), seq: 16 (over z, x, core), mp: 1.
Axes of the slice: x: 2, y: 2, z: 4, core: 2. Of those that a mesh axis runs over, the one named last changes fastest.
Arguments:
- student: bfloat16 [32768, 2048], P(('groups', 'seq'), 'mp'), parts along dimension 0, may hold values from -68 to 68
- teacher: bfloat16 [8192, 4096], P(('groups', 'seq'), 'mp'), parts along dimension 0, may hold values from -6 to 6
- weight: bfloat16 [4096, 2048], P('seq', 'mp'), may hold values from -0.09375 to 0.09375
- cotangent: bfloat16 [32768, 2048], P(('groups', 'seq'), 'mp'), parts along dimension 0, may hold values from -6 to 6
- block_map: int32 [256, 2], P('groups'), parts along dimension 0, may hold values from 0 to 31, as said below
- span_begin: int32 [32768], P(('groups', 'seq')), parts along dimension 0, may hold values from 0 to 255, as said below
- span_stop: int32 [32768], P(('groups', 'seq')), parts along dimension 0, may hold values from 1 to 256
Outputs:
- attended: bfloat16 [32768, 2048], P(('groups', 'seq'), 'mp'), parts along dimension 0
- student_grad: bfloat16 [32768, 2048], P(('groups', 'seq'), 'mp'), parts along dimension 0
- weight_grad: float32 [8192, 2048], P(('groups', 'seq'), 'mp'), parts along dimension 0
There are 2 independent parts, one for each index of `groups`. A program takes and returns all parts, laid end to end along the dimension named above; an argument that names none is the same for every part. Nothing has to cross between parts.
Inputs may be any that keep to these rules, and one draw needn't show every extreme that they name: `block_map`: teacher block m lies on teacher device m // 2. The student blocks of one device (1024 / 128 of them) name at most 1 block of one teacher device in all their entries together, and exactly 1 of some teacher device. An offset into the 256 key rows of the row's student block; span_begin < span_stop <= span_begin + 4.
All inputs are finite; a program needn't handle non-finite values.
Results may differ from a plain program's by a relative error of at most 0.007.
The roundings to bfloat16 on the way count: a program that leaves them out, or rounds other values in their place, can miss the bound.
Values may be sent and summed in bfloat16 or wider, within the bound.
A program may use at most 192 MiB of HBM per device.

v0:
```python
import jax
import jax.numpy as jnp
from jax import lax
from jax.sharding import PartitionSpec as P

HEAD = 128
BLK = 128
NB = 2


SCORE_FLOOR = -1e30


def attention_pass(queries, key_rows, grad_out, span_first, span_last, score_scale):
    position = jnp.arange(key_rows.shape[1])
    inside = (position[None, None, :] >= span_first[:, :, None]) & (
        position[None, None, :] < span_last[:, :, None]
    )
    inside = inside[:, None, :, :]
    scores = (
        jnp.einsum("bihd,bjhd->bhij", queries, key_rows, preferred_element_type=jnp.float32)
        * score_scale
    )
    scores = jnp.where(inside, scores, SCORE_FLOOR)
    row_max = jnp.max(scores, axis=3, keepdims=True)
    raised = jnp.where(inside, jnp.exp(scores - row_max), 0.0)
    attention = raised / jnp.sum(raised, axis=3, keepdims=True)
    attention_low = attention.astype(jnp.bfloat16)
    output = jnp.einsum(
        "bhij,bjhd->bihd", attention_low, key_rows, preferred_element_type=jnp.float32
    ).astype(jnp.bfloat16)
    pulled = jnp.einsum("bihd,bjhd->bhij", grad_out, key_rows, preferred_element_type=jnp.float32)
    centre = jnp.sum(attention * pulled, axis=3, keepdims=True)
    score_grad = (attention * (pulled - centre) * score_scale).astype(jnp.bfloat16)
    grad_query = jnp.einsum(
        "bhij,bjhd->bihd", score_grad, key_rows, preferred_element_type=jnp.float32
    ).astype(jnp.bfloat16)
    grad_keys = (
        jnp.einsum("bhij,bihd->bjhd", score_grad, queries, preferred_element_type=jnp.float32)
        + jnp.einsum("bhij,bihd->bjhd", attention_low, grad_out, preferred_element_type=jnp.float32)
    ).astype(jnp.bfloat16)
    return (output, grad_query, grad_keys)


def body(student, teacher, weight, cotangent, block_map, span_begin, span_stop):
    seq_count = lax.axis_size("seq")
    device_index = lax.axis_index("seq")
    student_rows, head_width = student.shape
    teacher_rows = teacher.shape[0]
    local_count = teacher_rows // BLK
    query_blocks = student_rows // BLK
    requests = query_blocks * NB
    slot_count = max(1, (requests + seq_count - 1) // seq_count)
    head_count = head_width // HEAD
    score_scale = HEAD ** (-0.5)
    features = lax.all_gather(teacher, "mp", axis=1, tiled=True)
    columns = features
    projected = jnp.dot(
        columns,
        lax.all_gather(weight, "seq", axis=0, tiled=True),
        preferred_element_type=jnp.float32,
    ).astype(jnp.bfloat16)
    all_requests = block_map.reshape(seq_count, requests)
    holder = all_requests // local_count
    local_block = all_requests % local_count
    earlier = jnp.arange(requests)[:, None] > jnp.arange(requests)[None, :]
    matches = holder[:, :, None] == holder[:, None, :]
    slot_rank = jnp.sum(matches & earlier[None, :, :], axis=2)
    slot_ids = jnp.arange(slot_count)
    chosen = (holder[:, None, :] == device_index) & (
        slot_rank[:, None, :] == slot_ids[None, :, None]
    )
    filled = jnp.any(chosen, axis=2)
    source_block = jnp.sum(jnp.where(chosen, local_block[:, None, :], 0), axis=2)
    own_blocks = projected.reshape(local_count, BLK, head_width)
    outgoing = jnp.where(
        filled[:, :, None, None],
        jnp.take(own_blocks, source_block, axis=0),
        jnp.zeros((), jnp.bfloat16),
    )
    incoming = lax.all_to_all(outgoing, "seq", split_axis=0, concat_axis=0, tiled=True)
    mine_holder = lax.dynamic_index_in_dim(holder, device_index, 0, keepdims=False)
    mine_rank = lax.dynamic_index_in_dim(slot_rank, device_index, 0, keepdims=False)
    slot_index = mine_holder * slot_count + mine_rank
    key_rows = jnp.take(
        incoming.reshape(seq_count * slot_count, BLK, head_width), slot_index, axis=0
    )
    key_rows = key_rows.reshape(query_blocks, NB * BLK, head_count, HEAD)
    output, grad_query, grad_keys = attention_pass(
        student.reshape(query_blocks, BLK, head_count, HEAD),
        key_rows,
        cotangent.reshape(query_blocks, BLK, head_count, HEAD),
        span_begin.reshape(query_blocks, BLK),
        span_stop.reshape(query_blocks, BLK),
        score_scale,
    )
    placement = (jnp.arange(seq_count * slot_count)[:, None] == slot_index[None, :]).astype(
        jnp.bfloat16
    )
    returning = jnp.einsum(
        "sr,rbd->sbd",
        placement,
        grad_keys.reshape(requests, BLK, head_width),
        preferred_element_type=jnp.float32,
    ).astype(jnp.bfloat16)
    returned = lax.all_to_all(
        returning.reshape(seq_count, slot_count, BLK, head_width),
        "seq",
        split_axis=0,
        concat_axis=0,
        tiled=True,
    )
    collect = (
        filled[None, :, :] & (source_block[None, :, :] == jnp.arange(local_count)[:, None, None])
    ).astype(jnp.bfloat16)
    projected_grad = jnp.einsum(
        "lsc,scbd->lbd", collect, returned, preferred_element_type=jnp.float32
    ).reshape(teacher_rows, head_width)
    grad_high = projected_grad.astype(jnp.bfloat16)
    grad_low = (projected_grad - grad_high.astype(jnp.float32)).astype(jnp.bfloat16)
    features_back = lax.all_gather(teacher, "mp", axis=1, tiled=True)
    columns = features_back
    dims = (((0,), (0,)), ((), ()))
    upper = lax.dot_general(columns, grad_high, dims, preferred_element_type=jnp.float32)
    lower = lax.dot_general(columns, grad_low, dims, preferred_element_type=jnp.float32)
    weight_grad = lax.psum_scatter(upper + lower, "seq", scatter_dimension=0, tiled=True)
    return (
        output.reshape(student_rows, head_width),
        grad_query.reshape(student_rows, head_width),
        weight_grad,
    )


def solution(mesh):
    in_specs = (
        P(("groups", "seq"), "mp"),
        P(("groups", "seq"), "mp"),
        P("seq", "mp"),
        P(("groups", "seq"), "mp"),
        P("groups", None),
        P(("groups", "seq")),
        P(("groups", "seq")),
    )
    out_specs = (P(("groups", "seq"), "mp"), P(("groups", "seq"), "mp"), P(("groups", "seq"), "mp"))
    return jax.shard_map(body, mesh=mesh, in_specs=in_specs, out_specs=out_specs, check_vma=False)
```

profile of v0, /device:TPU:0, one launch (start us, length us, event | category | flops | bytes accessed | tf_op | source)
XLA Modules:
  0.0 1101.6 jit_solution(10267654875906747012)
XLA Ops:
  7.2 0.0 copy-start
  7.2 0.0 all-gather.2.cloned.1.call-start
  7.2 0.7 all-gather.2.cloned.1.call-update
  7.9 0.8 copy.60
  8.7 0.1 reshape.405
  8.8 0.1 reshape.406
  8.9 0.4 convert_reduce_fusion
  9.3 0.1 fusion.61
  9.5 0.0 copy-start.2
  9.5 0.1 fusion.39
  9.6 0.0 copy-start.6
  9.6 0.5 copy-done.6
  10.1 129.7 %all-gather.2.cloned.1.call-done = bf16[4096,2048]{1,0:T(8,128)(2,1)} async-done(((bf16[256,2048]{1,0:T(8,128)(2,1)}), bf16[4096,2048]{1,0:T(8,128)(2,1)}) %all-gather.2.cloned.1.call-update) | async-done | bytes 16777232 | tf_op jit(solution)/shard_map/all_gather | solution.py:60
  139.8 0.0 copy-done
  139.8 8.3 convolution_convert_fusion
  148.1 4.6 gather_fusion
  152.7 0.0 copy-done.2
  152.7 7.6 fusion.8
  160.2 4.7 all-to-all-start
  165.0 0.0 reduce-scatter.2.cloned.1.call-start
  165.0 0.5 broadcast.404
  165.6 0.7 fusion.60
  166.2 0.1 add.110
  166.3 0.1 copy.61
  166.4 0.0 copy-start.1
  166.4 0.0 copy-start.4
  166.4 0.0 copy-start.5
  166.4 5.8 copy.86
  172.2 0.0 copy-done.1
  172.2 3.4 copy.84
  175.6 0.1 broadcast_bitcast_fusion
  175.7 0.0 copy-done.4
  175.7 0.0 copy-done.5
  175.7 0.2 fusion.35
  175.9 139.7 %all-to-all-done = bf16[16,1,128,2048]{3,2,1,0:T(8,128)(2,1)} async-done(((bf16[16,1,128,2048]{3,2,1,0:T(8,128)(2,1)}), bf16[16,1,128,2048]{3,2,1,0:T(8,128)(2,1)}, u32[]{:S(2)}, u32[]{:S(2)}) %all-to-all-start) | async-done | bytes 8388640 | tf_op jit(solution)/shard_map/all_to_all | solution.py:81
  315.6 8.4 gather_fusion.1
  324.0 9.8 copy.83
  333.8 8.0 bitcast_select_fusion.4
  341.8 12.6 %fusion.16 = f32[8,16,256,128]{3,2,1,0:T(8,128)} fusion(bf16[8,256,16,128]{3,2,1,0:T(8,128)(2,1)} %bitcast_select_fusion.4, bf16[8,128,16,128]{3,2,1,0:T(8,128)(2,1)} %bitcast.117), kind=kOutput, calls=%fused_computation.28 | convolution fusion | flops 1073741824 | bytes 29360128 | tf_op jit(solution)/shard_map/bihd,bjhd->bhij/dot_general | solution.py:32
  354.4 12.6 %fusion.18 = f32[8,16,256,128]{3,2,1,0:T(8,128)} fusion(bf16[8,256,16,128]{3,2,1,0:T(8,128)(2,1)} %bitcast_select_fusion.4, bf16[8,128,16,128]{3,2,1,0:T(8,128)(2,1)} %bitcast.119), kind=kOutput, calls=%fused_computation.30 | convolution fusion | flops 1073741824 | bytes 29360128 | tf_op jit(solution)/shard_map/bihd,bjhd->bhij/dot_general | solution.py:21
  367.1 19.9 %fusion.62 = (f32[8,16,128]{2,1,0:T(8,128)S(1)}, f32[8,16,128,256]{2,3,1,0:T(8,128)}) fusion(f32[8,16,256,128]{3,2,1,0:T(8,128)} %fusion.18, pred[8,128,256]{1,2,0:T(8,128)(4,1)S(1)} %fusion.35), kind=kOutput, calls=%fused_computation.103 | output fusion | flops 29360384 | bytes 33882112 | tf_op jit(solution)/shard_map/sub | solution.py:26
  387.0 32.6 %fusion.20 = f32[8,16,256,128]{3,2,1,0:T(8,128)} fusion(f32[8,16,256,128]{3,2,1,0:T(8,128)} %fusion.16, bf16[8,128,16,128]{3,2,1,0:T(8,128)(2,1)} %bitcast.120, f32[8,16,128,256]{2,3,1,0:T(8,128)} %get-tuple-element.22, f32[8,16,128]{2,1,0:T(8,128)S(1)} %get-tuple-element.21), kind=kOutput, calls=%fused_computation.32 | convolution fusion | flops 1103118592 | bytes 54591488 | tf_op jit(solution)/shard_map/bhij,bihd->bjhd/dot_general | solution.py:39
  419.6 17.4 %fusion.24 = bf16[8,256,16,128]{3,1,2,0:T(8,128)(2,1)} fusion(f32[8,16,256,128]{3,2,1,0:T(8,128)} %fusion.20, bf16[8,128,16,128]{3,2,1,0:T(8,128)(2,1)} %bitcast.118, f32[8,16,128,256]{2,3,1,0:T(8,128)} %get-tuple-element.22, f32[8,16,128]{2,1,0:T(8,128)S(1)} %get-tuple-element.21), kind=kOutput, calls=%fused_computation.34 | convolution fusion | flops 1090519040 | bytes 46202880 | tf_op jit(solution)/shard_map/bhij,bihd->bjhd/dot_general | solution.py:40
  437.0 12.0 %copy.75 = bf16[8,256,16,128]{3,2,1,0:T(8,128)(2,1)} copy(bf16[8,256,16,128]{3,1,2,0:T(8,128)(2,1)} %fusion.24) | data formatting | bytes 16777216 | tf_op jit(solution)/shard_map/convert_element_type | solution.py:41
  449.0 13.4 %reshape.413 = bf16[16,128,2048]{2,1,0:T(8,128)(2,1)} reshape(bf16[8,256,16,128]{3,2,1,0:T(8,128)(2,1)} %copy.75) | data formatting | bytes 16777216 | tf_op jit(solution)/shard_map/reshape | solution.py:103
  462.4 16.1 %convert_bitcast_fusion = bf16[16,1,128,2048]{3,0,2,1:T(8,128)(2,1)} fusion(bf16[16,128,2048]{2,1,0:T(8,128)(2,1)} %reshape.413, s32[16]{0:T(128)S(1)} %bitcast.127), kind=kOutput, calls=%fused_computation.22 | convolution fusion | flops 138412288 | bytes 16777280 | tf_op jit(solution)/shard_map/sr,rbd->sbd/dot_general | solution.py:100
  478.5 11.4 %copy.77 = bf16[16,1,128,2048]{3,2,1,0:T(8,128)(2,1)} copy(bf16[16,1,128,2048]{3,0,2,1:T(8,128)(2,1)} %convert_bitcast_fusion) | data formatting | bytes 16777216 | tf_op jit(solution)/shard_map/reshape | solution.py:107
  490.0 218.7 %all_to_all.10 = bf16[16,1,128,2048]{3,2,1,0:T(8,128)(2,1)S(1)} all-to-all(bf16[16,1,128,2048]{3,2,1,0:T(8,128)(2,1)} %copy.77), channel_id=1, replica_groups=mesh['groups'=2,'seq'=16,'mp'=1] {'seq'}, dimensions={0} | all-to-all | bytes 16777216 | tf_op jit(solution)/shard_map/all_to_all | solution.py:106
  708.7 0.0 copy-done.3
  708.7 0.0 copy-done.7
  708.7 9.4 fusion.6
  718.1 1.2 copy.79
  719.3 0.2 fusion.34
  719.5 13.5 %fusion.63 = f32[2048,4096]{1,0:T(8,128)} fusion(bf16[256,2048]{1,0:T(8,128)(2,1)S(1)} %get-tuple-element.16, bf16[256,4096]{1,0:T(8,128)(2,1)S(1)} %copy-done), kind=kOutput, calls=%fused_computation.104 | convolution fusion | flops 4294967296 | bytes 36700160 | tf_op jit(solution)/shard_map/dot_general | solution.py:124
  733.1 24.8 %add_bitcast_fusion = f32[4096,2048]{0,1:T(8,128)} fusion(f32[2048,4096]{1,0:T(8,128)} %fusion.63, bf16[256,2048]{1,0:T(8,128)(2,1)S(1)} %get-tuple-element.15, bf16[256,4096]{1,0:T(8,128)(2,1)S(1)} %copy-done), kind=kOutput, calls=%fused_computation.4 | convolution fusion | flops 4303355904 | bytes 70254592 | tf_op jit(solution)/shard_map/dot_general | solution.py:125
  757.9 0.0 reduce-scatter.2.cloned.1.call-update
  757.9 13.1 %copy.65 = bf16[8,256,16,128]{1,3,2,0:T(8,128)(2,1)} copy(bf16[8,256,16,128]{3,2,1,0:T(8,128)(2,1)} %bitcast_select_fusion.4) | data formatting | bytes 16777216 | tf_op jit(solution)/shard_map/jit(_take)/select_n | solution.py:85
  771.0 39.8 %convert_bitcast_fusion.1 = bf16[8,128,16,128]{1,3,2,0:T(8,128)(2,1)} fusion(bf16[8,256,16,128]{1,3,2,0:T(8,128)(2,1)} %copy.65, f32[8,16,256,128]{3,2,1,0:T(8,128)} %fusion.16, f32[8,16,128,256]{2,3,1,0:T(8,128)} %get-tuple-element.22, f32[8,16,128]{2,1,0:T(8,128)S(1)} %get-tuple-element.21), kind=kOutput, calls=%fused_computation.37 | convolution fusion | flops 1105215744 | bytes 46202880 | tf_op jit(solution)/shard_map/bhij,bjhd->bihd/dot_general | solution.py:35
  810.9 6.8 copy.72
  817.6 12.6 %convert_bitcast_fusion.2 = bf16[8,128,16,128]{1,3,2,0:T(8,128)(2,1)} fusion(bf16[8,256,16,128]{1,3,2,0:T(8,128)(2,1)} %copy.65, f32[8,16,128,256]{2,3,1,0:T(8,128)} %get-tuple-element.22, f32[8,16,128]{2,1,0:T(8,128)S(1)} %get-tuple-element.21), kind=kOutput, calls=%fused_computation.38 | convolution fusion | flops 1084227584 | bytes 29425664 | tf_op jit(solution)/shard_map/bhij,bjhd->bihd/dot_general | solution.py:29
  830.3 6.8 copy.67
  837.1 10.6 copy_bitcast_fusion
  847.6 244.0 %reduce-scatter.2.cloned.1.call-done = f32[256,2048]{0,1:T(8,128)} async-done(((f32[4096,2048]{0,1:T(8,128)}), f32[256,2048]{0,1:T(8,128)}) %reduce-scatter.2.cloned.1.call-update) | async-done | bytes 2097168 | tf_op jit(solution)/shard_map/reduce_scatter | solution.py:126
  1091.7 2.9 copy.80
  (10 shorter events, 0.1 us)
Async XLA Ops:
  7.2 132.6 %copy-start = (bf16[256,4096]{1,0:T(8,128)(2,1)S(1)}, bf16[256,4096]{1,0:T(8,128)(2,1)}, u32[]{:S(2)}) copy-start(bf16[256,4096]{1,0:T(8,128)(2,1)} %param.8) | copy-start | bytes 6291460
  7.2 132.6 %all-gather.2.cloned.1.call-start = ((), (), s32[]{:S(2)}) async-start(), calls=%async_computation.3 | async-start | bytes 17825792 | tf_op jit(solution)/shard_map/all_gather | solution.py:60
  9.5 143.2 %copy-start.2 = (pred[16]{0:T(512)(128)(4,1)}, pred[16]{0:T(512)(128)(4,1)S(1)}, u32[]{:S(2)}) copy-start(pred[16]{0:T(512)(128)(4,1)S(1)} %get-tuple-element.19) | copy-start | bytes 52
  9.6 0.5 copy-start.6
  160.2 155.4 %all-to-all-start = ((bf16[16,1,128,2048]{3,2,1,0:T(8,128)(2,1)}), bf16[16,1,128,2048]{3,2,1,0:T(8,128)(2,1)}, u32[]{:S(2)}, u32[]{:S(2)}) async-start(bf16[16,1,128,2048]{3,2,1,0:T(8,128)(2,1)} %fusion.8), calls=%async_computation | async-start | bytes 16777216 | tf_op jit(solution)/shard_map/all_to_all | solution.py:81
  165.0 926.7 %reduce-scatter.2.cloned.1.call-start = ((), (), s32[]{:S(2)}) async-start(), calls=%async_computation.4 | async-start | bytes 35651584 | tf_op jit(solution)/shard_map/reduce_scatter | solution.py:126
  166.4 5.8 copy-start.1
  166.4 9.3 copy-start.4
  166.4 9.3 copy-start.5
  490.0 218.8 %copy-start.3 = (pred[16]{0:T(512)(128)(4,1)S(1)}, pred[16]{0:T(512)(128)(4,1)}, u32[]{:S(2)}) copy-start(pred[16]{0:T(512)(128)(4,1)} %copy-done.2) | copy-start | bytes 52
  490.0 218.8 %copy-start.7 = (s32[16]{0:T(128)S(1)}, s32[16]{0:T(128)}, u32[]{:S(2)}) copy-start(s32[16]{0:T(128)} %copy-done.6) | copy-start | bytes 196
Sparse Core Ops, SparseCore 0:
  10.2 129.5 all-gather.1
  758.0 333.5 reduce-scatter.1
where the time goes:
time: 1110 us; the launch traced here: 1100 us
  waiting for transfers between devices  514 us (46%)
  blocking collectives  219 us (20%)
  matrix products  200 us (18%)
  local copies, waits for them, and re-layouts  112 us (10%)
  other arithmetic  37.4 us (3%)
  between operations  14.3 us (1%)
    reduce_scatter x1, waiting for transfers between devices, body(): lax.psum_scatter(upper + lower, 'seq', scatter_dimension=0, tiled=True)  244 us
    all_to_all x1, blocking collectives, body(): lax.all_to_all(returning.reshape(seq_count, slot_count, BLK, head_width),...  219 us
    all_to_all x1, waiting for transfers between devices, body(): lax.all_to_all(outgoing, 'seq', split_axis=0, concat_axis=0, tiled=True)  140 us
    all_gather x1, waiting for transfers between devices, body(): lax.all_gather(weight, 'seq', axis=0, tiled=True)  130 us
    dot_general x1, matrix products, attention_pass(): jnp.einsum('bhij,bjhd->bihd', score_grad, key_rows, preferred_element_typ...  39.8 us
    dot_general x1, matrix products, attention_pass(): jnp.einsum('bhij,bihd->bjhd', score_grad, queries, preferred_element_type...  32.6 us
    dot_general x1, matrix products, body(): lax.dot_general(columns, grad_low, dims, preferred_element_type=jnp.float32)  24.8 us
    unnamed x21, local copies, waits for them, and re-layouts  23.1 us
  transfers between devices with their start and end apart: 3, of which 3 were waited for; matrix products, arithmetic and copies ran while one was open for 9% of the time, Pallas kernels for 0%

commit v1 on v0

v1 whole, which is shorter than its diff:
```python
import functools

import jax
import jax.numpy as jnp
from jax import lax
from jax.experimental import pallas as pl
from jax.experimental.pallas import tpu as pltpu
from jax.sharding import PartitionSpec as P

HEAD = 128
BLK = 128
NB = 2
SUBS = 2
MESH = pl.DeviceIdType.MESH
SCORE_FLOOR = -1e30
VMEM_BYTES = 56 * 1024 * 1024


def ring_place(chips, snake, chip):
    if not snake:
        return chip
    z, x = chip // 2, chip % 2
    return z * (1 - x) + (chips - 1 - z) * x


def chip_at(chips, snake, place):
    if not snake:
        return place
    down = place // (chips // 2)
    return (1 - down) * (2 * place) + down * (2 * (chips - 1 - place) + 1)


def neighbours(chips, snake):
    me = lax.axis_index("seq")
    core = me % 2
    place = ring_place(chips, snake, me // 2)
    right = chip_at(chips, snake, (place + 1) % chips) * 2 + core
    left = chip_at(chips, snake, (place + chips - 1) % chips) * 2 + core
    sibling = me + 1 - 2 * core
    return me, core, place, (right, left), sibling


def enter(devices):
    barrier = pltpu.get_barrier_semaphore()
    for device in devices:
        pl.semaphore_signal(barrier, inc=1, device_id={"seq": device}, device_id_type=MESH)
    pl.semaphore_wait(barrier, len(devices))


def send(src, dst, send_sem, recv_sem, device):
    copy = pltpu.make_async_remote_copy(
        src_ref=src, dst_ref=dst, send_sem=send_sem, recv_sem=recv_sem,
        device_id={"seq": device}, device_id_type=MESH,
    )
    copy.start()
    return copy


def gather_kernel(chips, snake, x_ref, o_ref, own_sem, ring_send, ring_recv, pair_send, pair_recv):
    me, core, place, beside, sibling = neighbours(chips, snake)
    half = x_ref.shape[0] // 2
    part = half // SUBS
    enter((*beside, sibling))
    own = pltpu.make_async_copy(x_ref, o_ref.at[me], own_sem)
    own.start()
    ring, pair = {}, []
    for s in range(chips):
        for u in range(SUBS):
            for d in range(2):
                from_place = (place + chips - s) % chips if d == 0 else (place + s) % chips
                owner = chip_at(chips, snake, from_place) * 2 + core
                window = pl.ds(d * half + u * part, part)
                dst = o_ref.at[owner, window]
                src = x_ref.at[window] if s == 0 else dst
                if s > 0:
                    ring[d, s - 1, u].wait_recv()
                if s < chips - 1:
                    ring[d, s, u] = send(
                        src, dst, ring_send.at[d, s, u], ring_recv.at[d, s, u], beside[d]
                    )
                pair.append(
                    send(src, dst, pair_send.at[d, s, u], pair_recv.at[d, s, u], sibling)
                )
    own.wait()
    for copy in ring.values():
        copy.wait_send()
    for copy in pair:
        copy.wait()


def gather(x, chips, snake, collective_id):
    sems = [pltpu.SemaphoreType.DMA((2, chips, SUBS)) for _ in range(4)]
    return pl.pallas_call(
        functools.partial(gather_kernel, chips, snake),
        out_shape=jax.ShapeDtypeStruct((2 * chips, *x.shape), x.dtype),
        in_specs=[pl.BlockSpec(memory_space=pl.ANY)],
        out_specs=pl.BlockSpec(memory_space=pl.ANY),
        scratch_shapes=[pltpu.SemaphoreType.DMA, *sems],
        compiler_params=pltpu.CompilerParams(collective_id=collective_id, has_side_effects=True),
    )(x)


def reduce_kernel(
    chips, snake, x_ref, t_ref, o_ref, own, other, landed, landed_w, lhs, grads, term,
    own_sem, pair_send, pair_recv, ring_send, ring_recv, wide_send, wide_recv,
    t_sem, t_send, t_recv, g_send, g_recv,
):
    me, core, place, beside, sibling = neighbours(chips, snake)
    rows, width = x_ref.shape[1:]
    half = rows // 2
    part = half // SUBS
    enter((*beside, sibling))
    t_own = pltpu.make_async_copy(t_ref.at[core], lhs.at[core], t_sem)
    t_own.start()

    def target(d, s):
        if d == 0:
            return chip_at(chips, snake, (place + 2 * chips - 1 - s) % chips)
        return chip_at(chips, snake, (place + 1 + s) % chips)

    local, pair = {}, {}
    for s in range(chips):
        for d in range(2):
            window = pl.ds(d * half, half)
            local[d, s] = pltpu.make_async_copy(
                x_ref.at[target(d, s) * 2 + core, window], own.at[d, s], own_sem.at[d, s]
            )
            local[d, s].start()
            pair[d, s] = send(
                x_ref.at[target(d, s) * 2 + 1 - core, window], other.at[d, s],
                pair_send.at[d, s], pair_recv.at[d, s], sibling,
            )
    t_pair = send(t_ref.at[1 - core], lhs.at[core], t_send, t_recv, sibling)

    ring = {}
    for s in range(chips):
        for d in range(2):
            local[d, s].wait()
            pair[d, s].wait_recv()
        for u in range(SUBS):
            for d in range(2):
                if s > 0:
                    ring[d, s - 1, u].wait_recv()

                @pl.loop(0, part // 16)
                def _(i):
                    window = pl.ds(pl.multiple_of(u * part + i * 16, 16), 16)
                    total = own[d, s, window, :].astype(jnp.float32)
                    total = total + other[d, s, window, :].astype(jnp.float32)
                    if s > 0:
                        total = total + landed[d, s - 1, window, :].astype(jnp.float32)
                    if s < chips - 1:
                        own[d, s, window, :] = total.astype(jnp.bfloat16)
                    else:
                        place_in = pl.ds(pl.multiple_of(d * half + u * part + i * 16, 16), 16)
                        grads[core, place_in, :] = total.astype(jnp.bfloat16)

                window = pl.ds(u * part, part)
                if s < chips - 1:
                    ring[d, s, u] = send(
                        own.at[d, s, window], landed.at[d, s, window],
                        ring_send.at[d, s, u], ring_recv.at[d, s, u], beside[d],
                    )
    g_pair = send(grads.at[core], grads.at[core], g_send, g_recv, sibling)
    t_own.wait()
    t_pair.wait()
    g_pair.wait()
    for copy in ring.values():
        copy.wait_send()
    for copy in pair.values():
        copy.wait_send()

    deep = o_ref.shape[0]
    half = deep // 2
    part = half // SUBS
    tile = min(512, width)

    def make_term(d, s):
        chip = target(d, s)

        @pl.loop(0, width // tile)
        def _(j):
            columns = pl.ds(pl.multiple_of(j * tile, tile), tile)
            term[d, :, columns] = jnp.dot(
                lhs[0, chip, pl.ds(d * half, half), :], grads[0, :, columns],
                preferred_element_type=jnp.float32,
            ) + jnp.dot(
                lhs[1, chip, pl.ds(d * half, half), :], grads[1, :, columns],
                preferred_element_type=jnp.float32,
            )

    wide = {}
    for s in range(chips):
        for d in range(2):
            make_term(d, s)
        for u in range(SUBS):
            for d in range(2):
                if s > 0:
                    wide[d, s - 1, u].wait_recv()

                @pl.loop(0, part // 16)
                def _(i):
                    window = pl.ds(pl.multiple_of(u * part + i * 16, 16), 16)
                    total = term[d, window, :]
                    if s > 0:
                        total = total + landed_w[d, s - 1, window, :].astype(jnp.float32)
                    if s < chips - 1:
                        own[d, s, window, :] = total.astype(jnp.bfloat16)
                    else:
                        place_in = pl.ds(pl.multiple_of(d * half + u * part + i * 16, 16), 16)
                        o_ref[place_in, :] = total

                window = pl.ds(u * part, part)
                if s < chips - 1:
                    wide[d, s, u] = send(
                        own.at[d, s, window], landed_w.at[d, s, window],
                        wide_send.at[d, s, u], wide_recv.at[d, s, u], beside[d],
                    )
    for copy in wide.values():
        copy.wait_send()


def reduce(terms, features, deep, chips, snake, collective_id):
    _, rows, width = terms.shape
    lhs = features.reshape(rows, chips, 2, deep).transpose(2, 1, 3, 0)
    dma = pltpu.SemaphoreType.DMA
    return pl.pallas_call(
        functools.partial(reduce_kernel, chips, snake),
        out_shape=jax.ShapeDtypeStruct((deep, width), jnp.float32),
        in_specs=[pl.BlockSpec(memory_space=pl.ANY)] * 2,
        out_specs=pl.BlockSpec(memory_space=pltpu.VMEM),
        scratch_shapes=[
            pltpu.VMEM((2, chips, rows // 2, width), jnp.bfloat16),
            pltpu.VMEM((2, chips, rows // 2, width), jnp.bfloat16),
            pltpu.VMEM((2, chips - 1, rows // 2, width), jnp.bfloat16),
            pltpu.VMEM((2, chips - 1, deep // 2, width), jnp.bfloat16),
            pltpu.VMEM((2, chips, deep, rows), jnp.bfloat16),
            pltpu.VMEM((2, rows, width), jnp.bfloat16),
            pltpu.VMEM((2, deep // 2, width), jnp.float32),
            dma((2, chips)), dma((2, chips)), dma((2, chips)),
            dma((2, chips, SUBS)), dma((2, chips, SUBS)),
            dma((2, chips, SUBS)), dma((2, chips, SUBS)),
            dma, dma, dma, dma, dma,
        ],
        compiler_params=pltpu.CompilerParams(
            collective_id=collective_id, has_side_effects=True, vmem_limit_bytes=VMEM_BYTES
        ),
    )(terms, lhs)


def attention_kernel(
    picks, q_ref, c_ref, k0_ref, k1_ref, first_ref, last_ref, zeros_ref,
    out_ref, grad_ref, kg_ref, later,
):
    del picks, zeros_ref
    head_count = q_ref.shape[1] // HEAD
    scale = HEAD ** (-0.5)

    @pl.when(pl.program_id(1) == 0)
    def _():
        row = lax.broadcasted_iota(jnp.int32, (NB * BLK, BLK), 0)
        inside = (row >= first_ref[0]) & (row < last_ref[0])
        across = (((1,), (1,)), ((), ()))
        down = (((0,), (0,)), ((), ()))

        @pl.loop(0, head_count, unroll=2)
        def _(h):
            columns = pl.ds(pl.multiple_of(h * HEAD, HEAD), HEAD)
            q, c = q_ref[:, columns], c_ref[:, columns]
            both = jnp.concatenate([q, c], axis=0)
            keys = jnp.concatenate([k0_ref[0, :, columns], k1_ref[0, :, columns]], axis=0)
            products = lax.dot_general(keys, both, across, preferred_element_type=jnp.float32)
            scores = jnp.where(inside, products[:, :BLK] * scale, SCORE_FLOOR)
            raised = jnp.exp(scores - jnp.max(scores, axis=0, keepdims=True))
            probs = raised * (1.0 / jnp.sum(raised, axis=0, keepdims=True))
            pulled = products[:, BLK:]
            centre = jnp.sum(probs * pulled, axis=0, keepdims=True)
            score_grad = (probs * (pulled - centre) * scale).astype(jnp.bfloat16)
            weights = jnp.concatenate([score_grad, probs.astype(jnp.bfloat16)], axis=1)
            rows = lax.dot_general(weights, keys, down, preferred_element_type=jnp.float32)
            grad_ref[:, columns] = rows[:BLK].astype(jnp.bfloat16)
            out_ref[:, columns] = rows[BLK:].astype(jnp.bfloat16)
            key_grad = jnp.dot(weights, both, preferred_element_type=jnp.float32)
            key_grad = key_grad.astype(jnp.bfloat16)
            kg_ref[0, :, columns] = key_grad[:BLK]
            later[:, columns] = key_grad[BLK:]

    @pl.when(pl.program_id(1) == 1)
    def _():
        kg_ref[0] = later[...]


def attention(student, cotangent, blocks, picks, first, last):
    student_rows, width = student.shape
    query_blocks = student_rows // BLK
    rows = pl.BlockSpec((BLK, width), lambda b, n, picks: (b, 0))
    spans = pl.BlockSpec((1, 1, BLK), lambda b, n, picks: (b, 0, 0))
    return pl.pallas_call(
        attention_kernel,
        grid_spec=pltpu.PrefetchScalarGridSpec(
            num_scalar_prefetch=1,
            grid=(query_blocks, NB),
            in_specs=[
                rows,
                rows,
                pl.BlockSpec((1, BLK, width), lambda b, n, picks: (picks[NB * b], 0, 0)),
                pl.BlockSpec((1, BLK, width), lambda b, n, picks: (picks[NB * b + 1], 0, 0)),
                spans,
                spans,
                pl.BlockSpec(memory_space=pl.ANY),
            ],
            out_specs=[
                rows,
                rows,
                pl.BlockSpec((1, BLK, width), lambda b, n, picks: (picks[NB * b + n], 0, 0)),
            ],
            scratch_shapes=[pltpu.VMEM((BLK, width), jnp.bfloat16)],
        ),
        out_shape=[
            jax.ShapeDtypeStruct(student.shape, jnp.bfloat16),
            jax.ShapeDtypeStruct(student.shape, jnp.bfloat16),
            jax.ShapeDtypeStruct(blocks.shape, jnp.bfloat16),
        ],
        input_output_aliases={7: 2},
        compiler_params=pltpu.CompilerParams(
            dimension_semantics=("arbitrary", "arbitrary"), vmem_limit_bytes=VMEM_BYTES
        ),
    )(
        picks, student, cotangent, blocks, blocks,
        first.reshape(query_blocks, 1, BLK), last.reshape(query_blocks, 1, BLK),
        jnp.zeros(blocks.shape, jnp.bfloat16),
    )


def body(snake, student, teacher, weight, cotangent, block_map, span_begin, span_stop):
    seq_count = lax.axis_size("seq")
    chips = seq_count // 2
    device_index = lax.axis_index("seq")
    width = student.shape[1]
    teacher_rows = teacher.shape[0]
    query_blocks = student.shape[0] // BLK
    features = lax.all_gather(teacher, "mp", axis=1, tiled=True)
    deep = weight.shape[0]
    whole_weight = gather(weight, chips, snake, 1).reshape(seq_count * deep, width)
    projected = jnp.dot(features, whole_weight, preferred_element_type=jnp.float32)
    projected = projected.astype(jnp.bfloat16)
    blocks = gather(projected, chips, snake, 2).reshape(-1, BLK, width)
    picks = lax.dynamic_slice_in_dim(block_map, device_index * query_blocks, query_blocks, 0)
    output, grad_query, terms = attention(
        student, cotangent, blocks, picks.reshape(-1), span_begin, span_stop
    )
    weight_grad = reduce(
        terms.reshape(seq_count, teacher_rows, width), features, deep, chips, snake, 3
    )
    return output, grad_query, weight_grad


def solution(mesh):
    in_specs = (
        P(("groups", "seq"), "mp"),
        P(("groups", "seq"), "mp"),
        P("seq", "mp"),
        P(("groups", "seq"), "mp"),
        P("groups", None),
        P(("groups", "seq")),
        P(("groups", "seq")),
    )
    out_specs = (P(("groups", "seq"), "mp"), P(("groups", "seq"), "mp"), P(("groups", "seq"), "mp"))
    snake = mesh.shape["mp"] == 1
    return jax.shard_map(
        functools.partial(body, snake), mesh=mesh, in_specs=in_specs, out_specs=out_specs,
        check_vma=False,
    )
```

time: 1110 us -> 439 us (0.40)
  waiting for transfers between devices: 514 us -> 0 us
  Pallas kernels: 0 us -> 413 us
  blocking collectives: 219 us -> 0 us
  matrix products: 200 us -> 9.25 us
  local copies, waits for them, and re-layouts: 112 us -> 15.3 us
  other arithmetic: 37.4 us -> 0 us
  between operations: 14.3 us -> 0.69 us
    pallas_call x0 -> x4, Pallas kernels: none -> 413 us  [the longest x2 173 us: gather(): pl.pallas_call(functools.partial(gather_kernel, chips, snake), out_shape=...]
    reduce_scatter x1 -> x0, waiting for transfers between devices: 244 us -> none  [body(): lax.psum_scatter(upper + lower, 'seq', scatter_dimension=0, tiled=True)]
    all_to_all x1 -> x0, blocking collectives: 219 us -> none  [body(): lax.all_to_all(returning.reshape(seq_count, slot_count, BLK, head_width),...]
    dot_general x11 -> x1, matrix products: 200 us -> 9.25 us  [body(): jnp.dot(features, whole_weight, preferred_element_type=jnp.float32)]
    all_to_all x1 -> x0, waiting for transfers between devices: 140 us -> none  [body(): lax.all_to_all(outgoing, 'seq', split_axis=0, concat_axis=0, tiled=True)]
    all_gather x1 -> x0, waiting for transfers between devices: 130 us -> none  [body(): lax.all_gather(weight, 'seq', axis=0, tiled=True)]
    reshape x5 -> x2, local copies, waits for them, and re-layouts: 35.6 us -> 2.05 us  [the longest x1 1.46 us: reduce(): lhs = features.reshape(rows, chips, 2, deep).transpose(2, 1, 3, 0)]
    convert_element_type x3 -> x0, local copies, waits for them, and re-layouts: 25.5 us -> none  [the longest x1 12 us: attention_pass(): grad_keys = (jnp.einsum('bhij,bihd->bjhd', score_grad, queries, preferred...]
  transfers between devices with their start and end apart: 3 -> 0, of which waited for: 3 -> 0; matrix products, arithmetic and copies ran while one was open for 9% -> 0% of each run, Pallas kernels for 0% -> 0%
where the time goes in v1:
time: 439 us; the launch traced here: 438 us
  Pallas kernels  413 us (94%)
  local copies, waits for them, and re-layouts  15.3 us (3%)
  matrix products  9.25 us (2%)
    pallas_call x2, Pallas kernels, gather(): pl.pallas_call(functools.partial(gather_kernel, chips, snake), out_shape=...  173 us
    pallas_call x1, Pallas kernels, reduce(): pl.pallas_call(functools.partial(reduce_kernel, chips, snake), out_shape=...  173 us
    pallas_call x1, Pallas kernels, attention(): pl.pallas_call(attention_kernel, grid_spec=pltpu.PrefetchScalarGridSpec(n...  67.3 us
    dot_general x1, matrix products, body(): jnp.dot(features, whole_weight, preferred_element_type=jnp.float32)  9.25 us

profile of v1, /device:TPU:0, one launch (start us, length us, event | category | flops | bytes accessed | tf_op | source)
XLA Modules:
  0.0 438.5 jit_solution(9528983329206294478)
XLA Ops:
  0.6 0.0 copy-start
  0.7 0.7 copy-done
  1.3 0.1 constant_dynamic-slice_fusion
  1.4 0.1 copy.12
  1.5 0.6 reshape.27.picks
  2.1 0.0 copy-start.2
  2.1 86.9 %shard_map.94 = bf16[16,256,2048]{2,1,0:T(8,128)(2,1)} custom-call(bf16[256,2048]{1,0:T(8,128)(2,1)} %x_ref.1), custom_call_target="tpu_custom_call" | custom-call | tf_op jit(solution)/shard_map/pallas_call | solution.py:93
  89.0 0.0 copy-done.2
  89.0 9.3 %convolution_convert_fusion.x_ref = bf16[256,2048]{1,0:T(8,128)(2,1)} fusion(bf16[256,4096]{1,0:T(8,128)(2,1)S(1)} %copy-done.2, bf16[4096,2048]{1,0:T(8,128)(2,1)} %bitcast.14), kind=kOutput, calls=%fused_computation | convolution fusion | flops 4295491584 | bytes 19922944 | tf_op jit(solution)/shard_map/dot_general | solution.py:345
  98.2 86.1 %shard_map.95 = bf16[16,256,2048]{2,1,0:T(8,128)(2,1)} custom-call(bf16[256,2048]{1,0:T(8,128)(2,1)} %convolution_convert_fusion.x_ref), custom_call_target="tpu_custom_call" | custom-call | tf_op jit(solution)/shard_map/pallas_call | solution.py:93
  184.3 6.0 %broadcast_in_dim.3.zeros_ref = bf16[32,128,2048]{2,1,0:T(8,128)(2,1)} broadcast(bf16[]{:T(256)} %constant.4.clone.1), dimensions={} | broadcast | bytes 16777218 | tf_op jit(solution)/shard_map/broadcast_in_dim | solution.py:331
  190.3 67.3 %shard_map.96 = (bf16[1024,2048]{1,0:T(8,128)(2,1)}, bf16[1024,2048]{1,0:T(8,128)(2,1)}, bf16[32,128,2048]{2,1,0:T(8,128)(2,1)}) custom-call(s32[16]{0:T(128)} %reshape.27.picks, bf16[1024,2048]{1,0:T(8,128)(2,1)} %q_ref.1, bf16[1024,2048]{1,0:T(8,128)(2,1)} %c_ref.1, bf16[32,128,2048]{2,1,0:T(8,128)(2,1)} %bitcast.11, ...), custom_call_target="tpu_custom_call", output_to_operand_aliasing={{2}: (7, {})} | custom-call | tf_op jit(solution)/shard_map/pallas_call | solution.py:298
  257.6 3.3 copy.13
  260.9 1.5 copy.16
  262.4 0.0 copy-start.1
  262.4 173.0 %shard_map.97 = f32[256,2048]{1,0:T(8,128)} custom-call(bf16[16,256,2048]{2,1,0:T(8,128)(2,1)} %bitcast.13, bf16[2,8,256,256]{3,2,1,0:T(8,128)(2,1)} %bitcast.15), custom_call_target="tpu_custom_call" | custom-call | tf_op jit(solution)/shard_map/pallas_call | solution.py:227
  435.3 3.1 copy.19
  438.5 0.0 copy-done.1
Async XLA Ops:
  0.6 0.7 copy-start
  2.1 86.9 %copy-start.2 = (bf16[256,4096]{1,0:T(8,128)(2,1)S(1)}, bf16[256,4096]{1,0:T(8,128)(2,1)}, u32[]{:S(2)}) copy-start(bf16[256,4096]{1,0:T(8,128)(2,1)} %param.8) | copy-start | bytes 6291460
  262.4 176.1 %copy-start.1 = (s32[128,2]{0,1:T(2,128)S(1)}, s32[128,2]{0,1:T(2,128)}, u32[]{:S(2)}) copy-start(s32[128,2]{0,1:T(2,128)} %param.11) | copy-start | bytes 3076

commit v2 on v1

--- a/solution.py
+++ b/solution.py
@@ -11,6 +11,7 @@
 BLK = 128
 NB = 2
 SUBS = 2
+UNROLL = (16, 4, 16)
 MESH = pl.DeviceIdType.MESH
 SCORE_FLOOR = -1e30
 VMEM_BYTES = 56 * 1024 * 1024
@@ -249,86 +250,145 @@
 
 
 def attention_kernel(
-    picks, q_ref, c_ref, k0_ref, k1_ref, first_ref, last_ref, zeros_ref,
-    out_ref, grad_ref, kg_ref, later,
+    picks, q_ref, c_ref, k0_ref, k1_ref, first_ref, last_ref,
+    out_ref, grad_ref, kg_ref, held, empty, products, weights, held_sem, empty_sem,
 ):
-    del picks, zeros_ref
     head_count = q_ref.shape[1] // HEAD
     scale = HEAD ** (-0.5)
-
-    @pl.when(pl.program_id(1) == 0)
+    step, steps = pl.program_id(0), pl.num_programs(0)
+    slot = step % 2
+    share = kg_ref.shape[0] // (picks.shape[0] // NB)
+
+    def leaving(at, n):
+        return pltpu.make_async_copy(
+            held.at[at % 2, n], kg_ref.at[picks[NB * at + n]], held_sem.at[at % 2, n]
+        )
+
+    def filling(m):
+        return pltpu.make_async_copy(empty, kg_ref.at[step * share + m], empty_sem.at[m])
+
+    def unread(m):
+        named = picks[0] == step * share + m
+        for i in range(1, picks.shape[0]):
+            named = named | (picks[i] == step * share + m)
+        return jnp.logical_not(named)
+
+    @pl.when(step == 0)
     def _():
-        row = lax.broadcasted_iota(jnp.int32, (NB * BLK, BLK), 0)
-        inside = (row >= first_ref[0]) & (row < last_ref[0])
-        across = (((1,), (1,)), ((), ()))
-        down = (((0,), (0,)), ((), ()))
-
-        @pl.loop(0, head_count, unroll=2)
-        def _(h):
-            columns = pl.ds(pl.multiple_of(h * HEAD, HEAD), HEAD)
-            q, c = q_ref[:, columns], c_ref[:, columns]
-            both = jnp.concatenate([q, c], axis=0)
-            keys = jnp.concatenate([k0_ref[0, :, columns], k1_ref[0, :, columns]], axis=0)
-            products = lax.dot_general(keys, both, across, preferred_element_type=jnp.float32)
-            scores = jnp.where(inside, products[:, :BLK] * scale, SCORE_FLOOR)
-            raised = jnp.exp(scores - jnp.max(scores, axis=0, keepdims=True))
-            probs = raised * (1.0 / jnp.sum(raised, axis=0, keepdims=True))
-            pulled = products[:, BLK:]
-            centre = jnp.sum(probs * pulled, axis=0, keepdims=True)
-            score_grad = (probs * (pulled - centre) * scale).astype(jnp.bfloat16)
-            weights = jnp.concatenate([score_grad, probs.astype(jnp.bfloat16)], axis=1)
-            rows = lax.dot_general(weights, keys, down, preferred_element_type=jnp.float32)
-            grad_ref[:, columns] = rows[:BLK].astype(jnp.bfloat16)
-            out_ref[:, columns] = rows[BLK:].astype(jnp.bfloat16)
-            key_grad = jnp.dot(weights, both, preferred_element_type=jnp.float32)
-            key_grad = key_grad.astype(jnp.bfloat16)
-            kg_ref[0, :, columns] = key_grad[:BLK]
-            later[:, columns] = key_grad[BLK:]
-
-    @pl.when(pl.program_id(1) == 1)
+        empty[...] = jnp.zeros_like(empty)
+
+    for m in range(share):
+        @pl.when(unread(m))
+        def _():
+            filling(m).start()
+
+    @pl.when(step >= 2)
     def _():
-        kg_ref[0] = later[...]
+        for n in range(NB):
+            leaving(step - 2, n).wait()
+
+    row = lax.broadcasted_iota(jnp.int32, (NB * BLK, BLK), 0)
+    inside = (row >= first_ref[0]) & (row < last_ref[0])
+    across = (((1,), (1,)), ((), ()))
+    down = (((0,), (0,)), ((), ()))
+
+    def columns_of(h):
+        return pl.ds(pl.multiple_of(h * HEAD, HEAD), HEAD)
+
+    def keys_of(h):
+        columns = columns_of(h)
+        return jnp.concatenate([k0_ref[0, :, columns], k1_ref[0, :, columns]], axis=0)
+
+    def rows_of(h):
+        columns = columns_of(h)
+        return jnp.concatenate([q_ref[:, columns], c_ref[:, columns]], axis=0)
+
+    @pl.loop(0, head_count, unroll=min(UNROLL[0], head_count))
+    def _(h):
+        products[h] = lax.dot_general(
+            keys_of(h), rows_of(h), across, preferred_element_type=jnp.float32
+        )
+
+    @pl.loop(0, head_count, unroll=min(UNROLL[1], head_count))
+    def _(h):
+        scores = jnp.where(inside, products[h, :, :BLK] * scale, SCORE_FLOOR)
+        raised = jnp.exp(scores - jnp.max(scores, axis=0, keepdims=True))
+        probs = raised * (1.0 / jnp.sum(raised, axis=0, keepdims=True))
+        pulled = products[h, :, BLK:]
+        centre = jnp.sum(probs * pulled, axis=0, keepdims=True)
+        weights[h, :, :BLK] = (probs * (pulled - centre) * scale).astype(jnp.bfloat16)
+        weights[h, :, BLK:] = probs.astype(jnp.bfloat16)
+
+    @pl.loop(0, head_count, unroll=min(UNROLL[2], head_count))
+    def _(h):
+        columns = columns_of(h)
+        rows = lax.dot_general(weights[h], keys_of(h), down, preferred_element_type=jnp.float32)
+        grad_ref[:, columns] = rows[:BLK].astype(jnp.bfloat16)
+        out_ref[:, columns] = rows[BLK:].astype(jnp.bfloat16)
+        key_grad = jnp.dot(weights[h], rows_of(h), preferred_element_type=jnp.float32)
+        key_grad = key_grad.astype(jnp.bfloat16)
+        held[slot, 0, :, columns] = key_grad[:BLK]
+        held[slot, 1, :, columns] = key_grad[BLK:]
+
+    for n in range(NB):
+        leaving(step, n).start()
+
+    for m in range(share):
+        @pl.when(unread(m))
+        def _():
+            filling(m).wait()
+
+    @pl.when(step == steps - 1)
+    def _():
+        for n in range(NB):
+            leaving(step, n).wait()
+
+    @pl.when((step == steps - 1) & (steps > 1))
+    def _():
+        for n in range(NB):
+            leaving(step - 1, n).wait()
 
 
 def attention(student, cotangent, blocks, picks, first, last):
     student_rows, width = student.shape
     query_blocks = student_rows // BLK
-    rows = pl.BlockSpec((BLK, width), lambda b, n, picks: (b, 0))
-    spans = pl.BlockSpec((1, 1, BLK), lambda b, n, picks: (b, 0, 0))
+    share = blocks.shape[0] // query_blocks
+    rows = pl.BlockSpec((BLK, width), lambda b, picks: (b, 0))
+    spans = pl.BlockSpec((1, 1, BLK), lambda b, picks: (b, 0, 0))
     return pl.pallas_call(
         attention_kernel,
         grid_spec=pltpu.PrefetchScalarGridSpec(
             num_scalar_prefetch=1,
-            grid=(query_blocks, NB),
+            grid=(query_blocks,),
             in_specs=[
                 rows,
                 rows,
-                pl.BlockSpec((1, BLK, width), lambda b, n, picks: (picks[NB * b], 0, 0)),
-                pl.BlockSpec((1, BLK, width), lambda b, n, picks: (picks[NB * b + 1], 0, 0)),
+                pl.BlockSpec((1, BLK, width), lambda b, picks: (picks[NB * b], 0, 0)),
+                pl.BlockSpec((1, BLK, width), lambda b, picks: (picks[NB * b + 1], 0, 0)),
                 spans,
                 spans,
-                pl.BlockSpec(memory_space=pl.ANY),
             ],
-            out_specs=[
-                rows,
-                rows,
-                pl.BlockSpec((1, BLK, width), lambda b, n, picks: (picks[NB * b + n], 0, 0)),
+            out_specs=[rows, rows, pl.BlockSpec(memory_space=pl.ANY)],
+            scratch_shapes=[
+                pltpu.VMEM((2, NB, BLK, width), jnp.bfloat16),
+                pltpu.VMEM((BLK, width), jnp.bfloat16),
+                pltpu.VMEM((width // HEAD, NB * BLK, 2 * BLK), jnp.float32),
+                pltpu.VMEM((width // HEAD, NB * BLK, 2 * BLK), jnp.bfloat16),
+                pltpu.SemaphoreType.DMA((2, NB)),
+                pltpu.SemaphoreType.DMA((share,)),
             ],
-            scratch_shapes=[pltpu.VMEM((BLK, width), jnp.bfloat16)],
         ),
         out_shape=[
             jax.ShapeDtypeStruct(student.shape, jnp.bfloat16),
             jax.ShapeDtypeStruct(student.shape, jnp.bfloat16),
             jax.ShapeDtypeStruct(blocks.shape, jnp.bfloat16),
         ],
-        input_output_aliases={7: 2},
         compiler_params=pltpu.CompilerParams(
-            dimension_semantics=("arbitrary", "arbitrary"), vmem_limit_bytes=VMEM_BYTES
+            dimension_semantics=("arbitrary",), vmem_limit_bytes=VMEM_BYTES
         ),
     )(
         picks, student, cotangent, blocks, blocks,
         first.reshape(query_blocks, 1, BLK), last.reshape(query_blocks, 1, BLK),
-        jnp.zeros(blocks.shape, jnp.bfloat16),
     )
 
 

time: 439 us -> 399 us (0.909)
  Pallas kernels: 413 us -> 380 us
  local copies, waits for them, and re-layouts: 15.3 us -> 9.3 us
    pallas_call x1, Pallas kernels: 67.3 us -> 33.9 us  [attention(): pl.pallas_call(attention_kernel, grid_spec=pltpu.PrefetchScalarGridSpec(n...]
    broadcast_in_dim x1 -> x0, local copies, waits for them, and re-layouts: 5.97 us -> none  [attention(): jnp.zeros(blocks.shape, jnp.bfloat16)]
where the time goes in v2:
time: 399 us
  Pallas kernels  380 us (95%)
  local copies, waits for them, and re-layouts  9.3 us (2%)
  matrix products  9.25 us (2%)
    pallas_call x2, Pallas kernels, gather(): pl.pallas_call(functools.partial(gather_kernel, chips, snake), out_shape=...  173 us
    pallas_call x1, Pallas kernels, reduce(): pl.pallas_call(functools.partial(reduce_kernel, chips, snake), out_shape=...  173 us
    pallas_call x1, Pallas kernels, attention(): pl.pallas_call(attention_kernel, grid_spec=pltpu.PrefetchScalarGridSpec(n...  33.9 us
    dot_general x1, matrix products, body(): jnp.dot(features, whole_weight, preferred_element_type=jnp.float32)  9.25 us

profile of v2, /device:TPU:0, one launch (start us, length us, event | category | flops | bytes accessed | tf_op | source)
XLA Modules:
  0.0 399.0 jit_solution(803708005676995281)
XLA Ops:
  0.6 0.0 copy-start
  0.7 0.7 copy-done
  1.3 0.1 constant_dynamic-slice_fusion
  1.4 0.1 copy.11
  1.5 0.6 reshape.27.picks
  2.1 0.0 copy-start.2
  2.1 86.9 %shard_map.94 = bf16[16,256,2048]{2,1,0:T(8,128)(2,1)} custom-call(bf16[256,2048]{1,0:T(8,128)(2,1)} %x_ref.1), custom_call_target="tpu_custom_call" | custom-call | tf_op jit(solution)/shard_map/pallas_call | solution.py:94
  89.0 0.0 copy-done.2
  89.0 9.3 %convolution_convert_fusion.x_ref = bf16[256,2048]{1,0:T(8,128)(2,1)} fusion(bf16[256,4096]{1,0:T(8,128)(2,1)S(1)} %copy-done.2, bf16[4096,2048]{1,0:T(8,128)(2,1)} %bitcast.14), kind=kOutput, calls=%fused_computation | convolution fusion | flops 4295491584 | bytes 19922944 | tf_op jit(solution)/shard_map/dot_general | solution.py:405
  98.2 86.1 %shard_map.95 = bf16[16,256,2048]{2,1,0:T(8,128)(2,1)} custom-call(bf16[256,2048]{1,0:T(8,128)(2,1)} %convolution_convert_fusion.x_ref), custom_call_target="tpu_custom_call" | custom-call | tf_op jit(solution)/shard_map/pallas_call | solution.py:94
  184.3 33.9 %shard_map.96 = (bf16[1024,2048]{1,0:T(8,128)(2,1)}, bf16[1024,2048]{1,0:T(8,128)(2,1)}, bf16[32,128,2048]{2,1,0:T(8,128)(2,1)}) custom-call(s32[16]{0:T(128)} %reshape.27.picks, bf16[1024,2048]{1,0:T(8,128)(2,1)} %q_ref.1, bf16[1024,2048]{1,0:T(8,128)(2,1)} %c_ref.1, bf16[32,128,2048]{2,1,0:T(8,128)(2,1)} %bitcast.11, bf16[32,128,2048]{2,1,0:T(8,128)(2,1)} %bitcast.12, ...), custom_call_target="tpu_custom_call" | custom-call | tf_op jit(solution)/shard_map/pallas_call | solution.py:358
  218.2 3.3 copy.12
  221.5 1.5 copy.15
  223.0 0.0 copy-start.1
  223.0 172.9 %shard_map.97 = f32[256,2048]{1,0:T(8,128)} custom-call(bf16[16,256,2048]{2,1,0:T(8,128)(2,1)} %bitcast.13, bf16[2,8,256,256]{3,2,1,0:T(8,128)(2,1)} %bitcast.15), custom_call_target="tpu_custom_call" | custom-call | tf_op jit(solution)/shard_map/pallas_call | solution.py:228
  395.9 3.1 copy.17
  399.0 0.0 copy-done.1
Async XLA Ops:
  0.6 0.7 copy-start
  2.1 86.9 %copy-start.2 = (bf16[256,4096]{1,0:T(8,128)(2,1)S(1)}, bf16[256,4096]{1,0:T(8,128)(2,1)}, u32[]{:S(2)}) copy-start(bf16[256,4096]{1,0:T(8,128)(2,1)} %param.8) | copy-start | bytes 6291460
  223.0 176.1 %copy-start.1 = (s32[128,2]{0,1:T(2,128)S(1)}, s32[128,2]{0,1:T(2,128)}, u32[]{:S(2)}) copy-start(s32[128,2]{0,1:T(2,128)} %param.11) | copy-start | bytes 3076

commit v3 on v2

--- a/solution.py
+++ b/solution.py
@@ -38,20 +38,20 @@
     right = chip_at(chips, snake, (place + 1) % chips) * 2 + core
     left = chip_at(chips, snake, (place + chips - 1) % chips) * 2 + core
     sibling = me + 1 - 2 * core
-    return me, core, place, (right, left), sibling
+    return me, core, place, ({"seq": right}, {"seq": left}), {"seq": sibling}
 
 
 def enter(devices):
     barrier = pltpu.get_barrier_semaphore()
     for device in devices:
-        pl.semaphore_signal(barrier, inc=1, device_id={"seq": device}, device_id_type=MESH)
+        pl.semaphore_signal(barrier, inc=1, device_id=device, device_id_type=MESH)
     pl.semaphore_wait(barrier, len(devices))
 
 
 def send(src, dst, send_sem, recv_sem, device):
     copy = pltpu.make_async_remote_copy(
         src_ref=src, dst_ref=dst, send_sem=send_sem, recv_sem=recv_sem,
-        device_id={"seq": device}, device_id_type=MESH,
+        device_id=device, device_id_type=MESH,
     )
     copy.start()
     return copy
@@ -87,6 +87,82 @@
         copy.wait_send()
     for copy in pair:
         copy.wait()
+
+
+def gather_common_kernel(
+    chips, snake, kept, x_ref, o_ref, own_sem, ring_send, ring_recv, pair_send, pair_recv,
+    hand_send, hand_recv,
+):
+    me, core, place, beside, sibling = neighbours(chips, snake)
+    group = lax.axis_index("groups")
+    across = {"groups": 1 - group}
+    half = x_ref.shape[0] // 2
+    given = (x_ref.shape[1] - kept) // 2
+    columns = (
+        pl.ds(0, kept),
+        pl.ds(pl.multiple_of(kept + group * given, 128), given),
+        pl.ds(pl.multiple_of(kept + (1 - group) * given, 128), given),
+    )
+    enter((*beside, sibling, across))
+    own = pltpu.make_async_copy(x_ref, o_ref.at[me], own_sem)
+    own.start()
+    ring, pair, hand = {}, [], {}
+
+    def ends(d, s, u):
+        from_place = (place + chips - s) % chips if d == 0 else (place + s) % chips
+        owner = chip_at(chips, snake, from_place) * 2 + core
+        rows = pl.ds(d * half, half)
+        dst = o_ref.at[owner, rows, columns[u]]
+        return (x_ref.at[rows, columns[u]] if s == 0 else dst), dst
+
+    def to_sibling(d, s, u):
+        src, dst = ends(d, s, u)
+        pair.append(send(src, dst, pair_send.at[d, s, u], pair_recv.at[d, s, u], sibling))
+
+    def handed(s):
+        for d in range(2):
+            if s > 0:
+                hand[d, s].wait_recv()
+            to_sibling(d, s, 2)
+
+    for s in range(chips):
+        for u in (1, 0):
+            for d in range(2):
+                src, dst = ends(d, s, u)
+                if s > 0:
+                    ring[d, s - 1, u].wait_recv()
+                if s < chips - 1:
+                    ring[d, s, u] = send(
+                        src, dst, ring_send.at[d, s, u], ring_recv.at[d, s, u], beside[d]
+                    )
+                if u == 1 and s > 0:
+                    hand[d, s] = send(src, dst, hand_send.at[d, s], hand_recv.at[d, s], across)
+                to_sibling(d, s, u)
+        if s > 0:
+            handed(s - 1)
+    handed(chips - 1)
+    own.wait()
+    for copy in ring.values():
+        copy.wait_send()
+    for copy in hand.values():
+        copy.wait_send()
+    for copy in pair:
+        copy.wait()
+
+
+def gather_common(x, chips, snake, kept, collective_id):
+    dma = pltpu.SemaphoreType.DMA
+    return pl.pallas_call(
+        functools.partial(gather_common_kernel, chips, snake, kept),
+        out_shape=jax.ShapeDtypeStruct((2 * chips, *x.shape), x.dtype),
+        in_specs=[pl.BlockSpec(memory_space=pl.ANY)],
+        out_specs=pl.BlockSpec(memory_space=pl.ANY),
+        scratch_shapes=[
+            dma, dma((2, chips, 2)), dma((2, chips, 2)), dma((2, chips, 3)), dma((2, chips, 3)),
+            dma((2, chips)), dma((2, chips)),
+        ],
+        compiler_params=pltpu.CompilerParams(collective_id=collective_id, has_side_effects=True),
+    )(x)
 
 
 def gather(x, chips, snake, collective_id):
@@ -401,7 +477,12 @@
     query_blocks = student.shape[0] // BLK
     features = lax.all_gather(teacher, "mp", axis=1, tiled=True)
     deep = weight.shape[0]
-    whole_weight = gather(weight, chips, snake, 1).reshape(seq_count * deep, width)
+    given = width // 128 * 5 // 16 * 128
+    if lax.axis_size("groups") == 2 and given > 0:
+        whole_weight = gather_common(weight, chips, snake, width - 2 * given, 1)
+    else:
+        whole_weight = gather(weight, chips, snake, 1)
+    whole_weight = whole_weight.reshape(seq_count * deep, width)
     projected = jnp.dot(features, whole_weight, preferred_element_type=jnp.float32)
     projected = projected.astype(jnp.bfloat16)
     blocks = gather(projected, chips, snake, 2).reshape(-1, BLK, width)

time: 399 us -> 380 us (0.952)
  Pallas kernels: 380 us -> 360 us
    pallas_call x2 -> x1, Pallas kernels: 173 us -> 86.1 us  [gather(): pl.pallas_call(functools.partial(gather_kernel, chips, snake), out_shape=...]
    pallas_call x0 -> x1, Pallas kernels: none -> 66.9 us  [gather_common(): pl.pallas_call(functools.partial(gather_common_kernel, chips, snake, kept...]
where the time goes in v3:
time: 380 us; the launch traced here: 379 us
  Pallas kernels  360 us (95%)
  local copies, waits for them, and re-layouts  9.3 us (2%)
  matrix products  9.25 us (2%)
    pallas_call x1, Pallas kernels, reduce(): pl.pallas_call(functools.partial(reduce_kernel, chips, snake), out_shape=...  173 us
    pallas_call x1, Pallas kernels, gather(): pl.pallas_call(functools.partial(gather_kernel, chips, snake), out_shape=...  86.1 us
    pallas_call x1, Pallas kernels, gather_common(): pl.pallas_call(functools.partial(gather_common_kernel, chips, snake, kept...  66.9 us
    pallas_call x1, Pallas kernels, attention(): pl.pallas_call(attention_kernel, grid_spec=pltpu.PrefetchScalarGridSpec(n...  33.8 us
    dot_general x1, matrix products, body(): jnp.dot(features, whole_weight, preferred_element_type=jnp.float32)  9.25 us

profile of v3, /device:TPU:0, one launch (start us, length us, event | category | flops | bytes accessed | tf_op | source)
XLA Modules:
  0.0 379.5 jit_solution(16173658318909809370)
XLA Ops:
  0.6 0.0 copy-start
  0.7 0.7 copy-done
  1.3 0.1 constant_dynamic-slice_fusion
  1.4 0.1 copy.11
  1.5 0.6 reshape.27.picks
  2.1 0.0 copy-start.2
  2.1 66.9 %shard_map.94 = bf16[16,256,2048]{2,1,0:T(8,128)(2,1)} custom-call(bf16[256,2048]{1,0:T(8,128)(2,1)} %x_ref.1), custom_call_target="tpu_custom_call" | custom-call | tf_op jit(solution)/shard_map/pallas_call | solution.py:155
  68.9 0.0 copy-done.2
  68.9 9.3 %convolution_convert_fusion.x_ref = bf16[256,2048]{1,0:T(8,128)(2,1)} fusion(bf16[256,4096]{1,0:T(8,128)(2,1)S(1)} %copy-done.2, bf16[4096,2048]{1,0:T(8,128)(2,1)} %bitcast.14), kind=kOutput, calls=%fused_computation | convolution fusion | flops 4295491584 | bytes 19922944 | tf_op jit(solution)/shard_map/dot_general | solution.py:486
  78.2 86.1 %shard_map.95 = bf16[16,256,2048]{2,1,0:T(8,128)(2,1)} custom-call(bf16[256,2048]{1,0:T(8,128)(2,1)} %convolution_convert_fusion.x_ref), custom_call_target="tpu_custom_call" | custom-call | tf_op jit(solution)/shard_map/pallas_call | solution.py:170
  164.3 33.8 %shard_map.96 = (bf16[1024,2048]{1,0:T(8,128)(2,1)}, bf16[1024,2048]{1,0:T(8,128)(2,1)}, bf16[32,128,2048]{2,1,0:T(8,128)(2,1)}) custom-call(s32[16]{0:T(128)} %reshape.27.picks, bf16[1024,2048]{1,0:T(8,128)(2,1)} %q_ref.1, bf16[1024,2048]{1,0:T(8,128)(2,1)} %c_ref.1, bf16[32,128,2048]{2,1,0:T(8,128)(2,1)} %bitcast.11, bf16[32,128,2048]{2,1,0:T(8,128)(2,1)} %bitcast.12, ...), custom_call_target="tpu_custom_call" | custom-call | tf_op jit(solution)/shard_map/pallas_call | solution.py:434
  198.1 3.3 copy.12
  201.4 1.5 copy.15
  202.9 0.0 copy-start.1
  202.9 173.4 %shard_map.97 = f32[256,2048]{1,0:T(8,128)} custom-call(bf16[16,256,2048]{2,1,0:T(8,128)(2,1)} %bitcast.13, bf16[2,8,256,256]{3,2,1,0:T(8,128)(2,1)} %bitcast.15), custom_call_target="tpu_custom_call" | custom-call | tf_op jit(solution)/shard_map/pallas_call | solution.py:304
  376.3 3.1 copy.17
  379.4 0.0 copy-done.1
Async XLA Ops:
  0.6 0.7 copy-start
  2.1 66.9 %copy-start.2 = (bf16[256,4096]{1,0:T(8,128)(2,1)S(1)}, bf16[256,4096]{1,0:T(8,128)(2,1)}, u32[]{:S(2)}) copy-start(bf16[256,4096]{1,0:T(8,128)(2,1)} %param.8) | copy-start | bytes 6291460
  202.9 176.6 %copy-start.1 = (s32[128,2]{0,1:T(2,128)S(1)}, s32[128,2]{0,1:T(2,128)}, u32[]{:S(2)}) copy-start(s32[128,2]{0,1:T(2,128)} %param.11) | copy-start | bytes 3076
